TPU v7x, 128 devices: a whole 4x4x4 slice. The times are simulated.
128 devices in a mesh: grp: 8 (over z, core), row: 16 (over x, y).
Axes of the slice: x: 4, y: 4, z: 4, core: 2. Of those that a mesh axis runs over, the one named last changes fastest.
Arguments:
- embeddings: bfloat16 [32768, 4096], P(('grp', 'row')), may hold values from -6 to 6
- member_order: int32 [32768], P(('grp', 'row')), may hold values from 0 to 8191, as said below
- member_count: int32 [4], replicated, may hold values from 2048 to 8192, as said below
Outputs:
- nearest: float32 [32768], P(('grp', 'row'))
Inputs may be any that keep to these rules, and one draw needn't show every extreme that they name: `member_order`: each cluster's 8192 slots carry every rank of 0 to 8191 once. `member_count`: one cluster is full.
All inputs are finite; a program needn't handle non-finite values.
Results may differ from a plain program's by a relative error of at most 0.0003.
Values may be sent and summed in bfloat16 or wider, within the bound.
A program may use at most 128 MiB of HBM per device.

v0:
```python
import jax
import jax.numpy as jnp
from jax import lax
from jax.sharding import PartitionSpec as P


def from_partner(value, axis, stride):
    mask = 2**stride
    pairs = [(source, source ^ mask) for source in range(lax.axis_size(axis))]
    return lax.ppermute(value, axis, pairs)


def shards(embeddings, member_order, member_count):
    rows = embeddings.shape[0]
    half_rows = lax.axis_size("row") * rows
    group_index = lax.axis_index("grp")
    row_index = lax.axis_index("row")
    cluster = group_index // 2
    side = group_index % 2
    values = embeddings.astype(jnp.float32)
    squares = jnp.sum(values * values, axis=1, keepdims=True)
    unit = (values * lax.rsqrt(squares + 1e-06)).astype(jnp.bfloat16)
    limit = member_count[cluster]
    my_slots = side * half_rows + row_index * rows + jnp.arange(rows, dtype=jnp.int32)
    live_here = my_slots < limit
    partner_unit, partner_order = from_partner((unit, member_order), "grp", 0)
    queries = jnp.concatenate([unit, partner_unit], axis=0)
    query_order = jnp.concatenate([member_order, partner_order], axis=0)
    key_base = side * half_rows
    initial = jnp.full((2 * rows,), -1.0, jnp.float32)
    piece_unit = lax.all_gather(unit, "row", axis=0, tiled=True)
    piece_order = lax.all_gather(member_order, "row", axis=0, tiled=True)
    scores = lax.dot_general(
        queries, piece_unit, (((1,), (1,)), ((), ())), preferred_element_type=jnp.float32
    )
    slots = key_base + jnp.arange(piece_unit.shape[0], dtype=jnp.int32)
    allowed = (slots < limit)[None, :] & (piece_order[None, :] < query_order[:, None])
    best = jnp.maximum(initial, jnp.max(jnp.where(allowed, scores, -1.0), axis=1))
    returned = from_partner(best[rows:], "grp", 0)
    result = jnp.maximum(best[:rows], returned)
    return jnp.where(live_here, result, jnp.float32(-1.0))


def solution(mesh):
    in_specs = (P(("grp", "row"), None), P(("grp", "row")), P())
    out_specs = P(("grp", "row"))
    return jax.shard_map(shards, mesh=mesh, in_specs=in_specs, out_specs=out_specs, check_vma=False)
```

profile of v0, /device:TPU:1, one launch (start us, length us, event | category | flops | bytes accessed | tf_op | source)
XLA Modules:
  0.0 244.9 jit_solution(8807569875550880838)
XLA Ops:
  6.5 0.0 copy-start
  6.5 0.0 copy-start.1
  6.5 0.0 all-gather.3.cloned.1.call-start
  6.5 2.1 fusion
  8.7 3.5 %fusion.1 = bf16[256,4096]{1,0:T(8,128)(2,1)} fusion(bf16[256,4096]{1,0:T(8,128)(2,1)} %param.3, f32[256]{0:T(256)S(1)} %add_rsqrt_fusion), kind=kLoop, calls=%fused_computation.4 | loop fusion | flops 3145728 | bytes 4195328 | tf_op jit(solution)/shard_map/convert_element_type | solution.py:22
  12.2 0.0 all-gather.3.cloned.1.call-update
  12.2 1.5 collective-permute-start.1
  13.7 0.0 copy-done
  13.7 0.1 collective-permute-start
  13.8 0.0 copy-done.1
  13.8 0.6 dynamic_slice.3
  14.4 0.6 add_compare_fusion
  15.0 19.0 %all-gather = s32[16,1,256]{2,1,0:T(1,128)S(1)} all-gather(s32[1,1,256]{2,1,0:T(1,128)S(1)} %bitcast.5), channel_id=1, replica_groups=mesh['grp'=8,'row'=16] {'row'}, dimensions={0}, use_global_device_ids=true | all-gather | bytes 17408 | tf_op jit(solution)/shard_map/all_gather | solution.py:32
  34.0 0.0 collective-permute-done
  34.1 0.0 collective-permute-done.1
  34.1 178.4 %all-gather.3.cloned.1.call-done = bf16[4096,4096]{1,0:T(8,128)(2,1)} async-done(((bf16[256,4096]{1,0:T(8,128)(2,1)}), bf16[4096,4096]{1,0:T(8,128)(2,1)}) %all-gather.3.cloned.1.call-update) | async-done | bytes 33554448 | tf_op jit(solution)/shard_map/all_gather | solution.py:31
  212.5 22.7 %select_reduce_fusion = f32[512]{0:T(512)S(1)} fusion(s32[4096]{0:T(1024)S(1)} %bitcast.4, s32[512]{0:T(512)S(1)} %pad_add_fusion, pred[4096]{0:T(1024)(128)(4,1)S(1)} %add_compare_fusion, bf16[4096,4096]{1,0:T(8,128)(2,1)} %all-gather.3.cloned.1.call-done, bf16[256,4096]{1,0:T(8,128)(2,1)S(1)} %collective-permute-done.1, bf16[256,4096]{1,0:T(8,128)(2,1)} %fusion.1), kind=kOutput, calls=%fused_computation | convolution fusion | flops 17196646400 | bytes 37773312 | tf_op jit(solution)/shard_map/dot_general | solution.py:33
  235.3 0.8 collective-permute-start.2
  236.0 0.8 collective-permute-done.2
  236.9 1.2 compare_select_fusion
  (4 shorter events, 0.0 us)
Async XLA Ops:
  6.5 7.2 %copy-start = (s32[256]{0:T(256)S(1)}, s32[256]{0:T(256)}, u32[]{:S(2)}) copy-start(s32[256]{0:T(256)} %param.4) | copy-start | bytes 3076
  6.5 7.3 %copy-start.1 = (s32[4]{0:T(128)S(1)}, s32[4]{0:T(128)}, u32[]{:S(2)}) copy-start(s32[4]{0:T(128)} %param.5) | copy-start | bytes 52
  6.5 205.9 %all-gather.3.cloned.1.call-start = ((), (), s32[]{:S(2)}) async-start(), calls=%async_computation | async-start | bytes 35651584 | tf_op jit(solution)/shard_map/all_gather | solution.py:31
  12.2 21.9 %collective-permute-start.1 = (bf16[256,4096]{1,0:T(8,128)(2,1)}, bf16[256,4096]{1,0:T(8,128)(2,1)S(1)}, u32[]{:S(2)}, u32[]{:S(2)}) collective-permute-start(bf16[256,4096]{1,0:T(8,128)(2,1)} %fusion.1), channel_id=1, source_target_pairs={{0,16},{16,0},{32,48},{48,32},{64,80},{80,64},{96,112},{112,96},{1... | collective-permute-start | bytes 6291464 | tf_op jit(solution)/shard_map/ppermute | solution.py:10
  13.7 20.4 %collective-permute-start = (s32[256]{0:T(256)S(1)}, s32[256]{0:T(256)S(1)}, u32[]{:S(2)}, u32[]{:S(2)}) collective-permute-start(s32[256]{0:T(256)S(1)} %copy-done), channel_id=1, source_target_pairs={{0,16},{16,0},{32,48},{48,32},{64,80},{80,64},{96,112},{112,96},{1... | collective-permute-start | bytes 3080 | tf_op jit(solution)/shard_map/ppermute | solution.py:10
  235.3 1.6 collective-permute-start.2
Sparse Core Ops, SparseCore 0:
  12.3 200.1 all-gather.2
where the time goes:
time: 245 us
  waiting for transfers between devices  179 us (73%)
  matrix products  22.7 us (9%)
  blocking collectives  19 us (8%)
  between operations  13.4 us (5%)
  other arithmetic  7.46 us (3%)
    all_gather x1, waiting for transfers between devices, shards(): piece_unit = lax.all_gather(unit, 'row', axis=0, tiled=True)  178 us
    dot_general x1, matrix products, shards(): lax.dot_general(queries, piece_unit, (((1,), (1,)), ((), ())), preferred_...  22.7 us
    all_gather x1, blocking collectives, shards(): piece_order = lax.all_gather(member_order, 'row', axis=0, tiled=True)  19 us
  transfers between devices with their start and end apart: 4, of which 2 were waited for; matrix products, arithmetic and copies ran while one was open for 1% of the time, Pallas kernels for 0%

commit v1 on v0

v1 whole, which is shorter than its diff:
```python
import jax
import jax.numpy as jnp
from jax import lax
from jax.experimental import pallas as pl
from jax.experimental.pallas import tpu as pltpu
from jax.sharding import PartitionSpec as P

MESH = pl.DeviceIdType.MESH
SIDE = 4
ROWS = 256
HALF = ROWS // 2
CHUNK = 64
CHUNKS = ROWS // CHUNK
EMPTY = 1 << 20
NEAR, FAR, OTHER = 4, 5, 6
SLOTS = 10


def kernel(
    rows_hbm, rank_ref, out_ref, blocks, rank_lane, rank_row, best_row, best_lane, mail, load_sem, send_sem, recv_sem,
    rank_send, rank_recv, mail_send, mail_recv,
):
    group, place = lax.axis_index("grp"), lax.axis_index("row")
    core = lax.rem(group, 2)
    x, y = place // SIDE, lax.rem(place, SIDE)

    def device(main, side, flip=False):
        dx = main * (1 - core) + side * core
        dy = main * core + side * (1 - core)
        there = lax.rem(x + dx + SIDE, SIDE) * SIDE + lax.rem(y + dy + SIDE, SIDE)
        return (group + 1 - 2 * core if flip else group, there)

    partner = device(0, 0, True)
    main_late = (x * (1 - core) + y * core) // 2
    side_late = (y * (1 - core) + x * core) // 2

    greeted = [device(i, 0) for i in (1, 2, 3)] + [device(0, i) for i in (1, 2, 3)]
    greeted += [partner] + [device(i, 0, True) for i in (1, 2, 3)] + [device(0, i, True) for i in (1, 2, 3)]
    barrier = pltpu.get_barrier_semaphore()
    for there in greeted:
        pl.semaphore_signal(barrier, inc=1, device_id=there, device_id_type=MESH)

    def load(c):
        at = pl.ds(c * CHUNK, CHUNK)
        return pltpu.make_async_copy(rows_hbm.at[at], blocks.at[0, at], load_sem.at[c])

    for c in range(CHUNKS):
        load(c).start()

    def normalise(c):
        load(c).wait()

        @pl.loop(0, CHUNK // 16)
        def _(i):
            at = pl.ds(pl.multiple_of(c * CHUNK + i * 16, 16), 16)
            values = blocks[0, at, :].astype(jnp.float32)
            squares = jnp.sum(values * values, axis=1, keepdims=True)
            blocks[0, at, :] = (values * lax.rsqrt(squares + 1e-06)).astype(jnp.bfloat16)

    def move(source, slot, c, there):
        at = pl.ds(c * CHUNK, CHUNK)
        return pltpu.make_async_remote_copy(
            blocks.at[source, at], blocks.at[slot, at], send_sem.at[slot, c], recv_sem.at[slot, c],
            device_id=there, device_id_type=MESH,
        )

    sent = []

    def send(source, slot, c, there):
        copy = move(source, slot, c, there)
        copy.start()
        sent.append(copy)

    def await_chunk(slot, c):
        move(slot, slot, c, partner).wait_recv()

    down, up, side_up = device(-1, 0), device(1, 0), device(0, 1)

    normalise(0)
    pl.semaphore_wait(barrier, len(greeted))
    rank_to = [(i, device(-i, 0)) for i in (1, 2, 3)] + [(NEAR, side_up), (FAR, device(0, 2))]
    rank_to += [(OTHER + i, device(-i, 0, True)) for i in range(4)]

    def rank_copy(slot, there):
        return pltpu.make_async_remote_copy(
            rank_lane.at[0], rank_lane.at[slot], rank_send.at[slot], rank_recv.at[slot], device_id=there, device_id_type=MESH
        )

    rank_lane[0] = rank_ref[...]
    for c in range(CHUNKS):
        if c:
            normalise(c)
        send(0, 1, c, down)
        send(0, NEAR, c, side_up)
        if c >= CHUNKS // 2:
            send(0, 3, c, up)
        send(0, OTHER, c, partner)
        if c == 0:
            for slot, there in rank_to:
                rank_copy(slot, there).start()

    best_row[...] = jnp.full_like(best_row, -1.0)
    best_lane[...] = jnp.full_like(best_lane, -1.0)

    def column(slot):
        for h in range(2):
            wide = jnp.broadcast_to(rank_lane[slot, h][:1], (HALF, HALF))
            rank_row[slot, pl.ds(h * HALF, HALF), :] = wide.T

    column(0)
    for slot, there in rank_to:
        rank_copy(slot, there).wait_recv()
    for slot, there in rank_to:
        column(slot)

    def meet(a, start, count, b, half, halves, both=True):
        left = blocks[a, pl.ds(start, count), :]
        right = blocks[b, pl.ds(pl.multiple_of(half * HALF, HALF), halves * HALF), :]
        scores = lax.dot_general(left, right, (((1,), (1,)), ((), ())), preferred_element_type=jnp.float32)
        mine = rank_row[a, pl.ds(start, count), :].reshape(count // 8, 8, HALF)
        best = best_row[a, pl.ds(start, count), :].reshape(count // 8, 8, HALF)
        for h in range(halves):
            part = scores[:, h * HALF : (h + 1) * HALF].reshape(count // 8, 8, HALF)
            earlier = rank_lane[b, half + h][None] < mine
            best = jnp.maximum(best, jnp.where(earlier, part, -1.0))
            if both:
                back = jnp.max(jnp.where(earlier, -1.0, part), axis=0)
                best_lane[b, half + h] = jnp.maximum(best_lane[b, half + h], back)
        best_row[a, pl.ds(start, count), :] = best.reshape(count, HALF)

    def meet_each(a, start, count, first, last):
        @pl.loop(first, last)
        def _(b):
            meet(a, start, count, b, 0, 2)

    def quarter(a, h, b, swap):
        meet(a, h * HALF, HALF, b, h + swap - 2 * h * swap, 1)

    def crossed(a, swap):
        quarter(a, 0, a + OTHER, swap)
        quarter(a, 1, a + OTHER, swap)

    def await_main(k):
        slot, c = 1 + k // CHUNKS, k % CHUNKS
        await_chunk(slot, c)
        if k < CHUNKS + CHUNKS // 2:
            send(slot, slot + 1, c, down)
        send(slot, slot + OTHER, c, partner)

    def await_side(k):
        slot, c = NEAR + k // CHUNKS, k % CHUNKS
        await_chunk(slot, c)
        if k < CHUNKS:
            send(slot, FAR, c, side_up)

    def await_other(slot, first=0, last=CHUNKS):
        for c in range(first, last):
            await_chunk(OTHER + slot, c)

    @pl.loop(0, 2)
    def _(h):
        meet(0, pl.multiple_of(h * HALF, HALF), HALF, 0, 0, 2, both=False)

    await_main(0)
    await_other(0)
    crossed(0, core)
    await_main(1)
    for b in (0, OTHER):
        meet(1, 0, HALF, b, 0, 2)
    await_main(2)
    await_side(0)
    await_main(3)
    await_side(1)
    for b in (0, OTHER):
        meet(1, HALF, HALF, b, 0, 2)
    meet_each(NEAR, 0, HALF, 0, 2)
    await_main(4)
    await_side(2)
    await_chunk(3, 2)
    send(3, 3 + OTHER, 2, partner)
    await_other(1)
    crossed(1, core)
    await_main(5)
    await_side(3)
    await_chunk(3, 3)
    send(3, 3 + OTHER, 3, partner)
    meet_each(NEAR, HALF, HALF, 0, 2)
    meet_each(2, 0, HALF, OTHER, OTHER + 2)
    quarter(2, 0, 0, main_late)
    await_main(6)
    await_side(4)
    meet(2, 0, HALF, NEAR, 0, 2)
    meet_each(3, HALF, HALF, OTHER, OTHER + 2)
    meet(3, HALF, HALF, NEAR, 0, 2)
    await_main(7)
    await_side(5)
    meet_each(2, HALF, HALF, OTHER, OTHER + 2)
    quarter(2, 1, 0, main_late)
    meet(2, HALF, HALF, NEAR, 0, 2)
    await_main(8)
    await_side(6)

    @pl.loop(0, 3)
    def _(b):
        quarter(FAR, 0, b, side_late)

    await_other(2)
    crossed(2, core)
    meet(3, HALF, HALF, OTHER + 2, 0, 2)
    meet_each(3, 0, CHUNK, OTHER, OTHER + 3)
    meet(3, 0, CHUNK, NEAR, 0, 2)
    await_main(9)
    await_side(7)
    meet_each(3, CHUNK, CHUNK, OTHER, OTHER + 3)
    meet(3, CHUNK, CHUNK, NEAR, 0, 2)

    @pl.loop(0, 3)
    def _(b):
        quarter(FAR, 1, b, side_late)

    quarter(FAR, 0, 3, side_late)
    quarter(FAR, 1, 3, side_late)
    await_other(3)
    crossed(3, core)

    def finish(slot):
        for h in range(2):
            turned = best_row[slot, pl.ds(h * HALF, HALF), :].T
            found = jnp.max(turned.reshape(HALF // 8, 8, HALF), axis=0)
            mail[slot, h] = jnp.maximum(found, best_lane[slot, h])

    owners = [(i, device(i, 0)) for i in (1, 2, 3)] + [(NEAR, device(0, -1)), (FAR, device(0, -2))]
    owners += [(OTHER + i, device(0, i, True)) for i in range(4)]

    def mail_copy(slot, there):
        return pltpu.make_async_remote_copy(
            mail.at[slot], mail.at[SLOTS + slot], mail_send.at[slot], mail_recv.at[slot], device_id=there, device_id_type=MESH
        )

    for slot, there in owners:
        finish(slot)
        mail_copy(slot, there).start()
    finish(0)
    found = mail[0]
    for slot, there in owners:
        mail_copy(slot, there).wait_recv()
        found = jnp.maximum(found, mail[SLOTS + slot])
    found = jnp.max(found, axis=1)
    out_ref[...] = jnp.where(rank_ref[:, 0, :] < EMPTY, found, -1.0)

    for copy in sent:
        copy.wait_send()
    for slot, there in rank_to:
        rank_copy(slot, there).wait_send()
    for slot, there in owners:
        mail_copy(slot, there).wait_send()


def shards(embeddings, member_order, member_count):
    rows, depth = embeddings.shape
    group, place = lax.axis_index("grp"), lax.axis_index("row")
    base = (group % 2) * lax.axis_size("row") * rows + place * rows
    live = base + jnp.arange(rows, dtype=jnp.int32) < member_count[group // 2]
    rank = jnp.where(live, member_order, EMPTY).reshape(2, 1, HALF)
    rank = jnp.broadcast_to(rank, (2, 8, HALF))
    copies = [pltpu.SemaphoreType.DMA((SLOTS, CHUNKS))] * 2
    letters = [pltpu.SemaphoreType.DMA((SLOTS,))] * 4
    best = pl.pallas_call(
        kernel,
        out_shape=jax.ShapeDtypeStruct((2, HALF), jnp.float32),
        in_specs=[pl.BlockSpec(memory_space=pl.ANY), pl.BlockSpec(memory_space=pltpu.VMEM)],
        out_specs=pl.BlockSpec(memory_space=pltpu.VMEM),
        scratch_shapes=[
            pltpu.VMEM((SLOTS, rows, depth), jnp.bfloat16),
            pltpu.VMEM((SLOTS, 2, 8, HALF), jnp.int32),
            pltpu.VMEM((SLOTS, rows, HALF), jnp.int32),
            pltpu.VMEM((SLOTS, rows, HALF), jnp.float32),
            pltpu.VMEM((SLOTS, 2, 8, HALF), jnp.float32),
            pltpu.VMEM((2 * SLOTS, 2, 8, HALF), jnp.float32),
            pltpu.SemaphoreType.DMA((CHUNKS,)),
            *copies,
            *letters,
        ],
        compiler_params=pltpu.CompilerParams(collective_id=0, has_side_effects=True, vmem_limit_bytes=48 * 2**20),
        name="nearest_earlier",
    )(embeddings, rank)
    return best.reshape(rows)


def solution(mesh):
    in_specs = (P(("grp", "row"), None), P(("grp", "row")), P())
    out_specs = P(("grp", "row"))
    return jax.shard_map(shards, mesh=mesh, in_specs=in_specs, out_specs=out_specs, check_vma=False)
```

time: 245 us -> 80.4 us (0.33)
  waiting for transfers between devices: 179 us -> 0 us
  Pallas kernels: 0 us -> 75.5 us
  matrix products: 22.7 us -> 0 us
  blocking collectives: 19 us -> 0 us
  between operations: 13.4 us -> 0.01 us
  other arithmetic: 7.46 us -> 1.33 us
  local copies, waits for them, and re-layouts: 0.62 us -> 3.4 us
    all_gather x1 -> x0, waiting for transfers between devices: 178 us -> none  [shards(): piece_unit = lax.all_gather(unit, 'row', axis=0, tiled=True)]
    pallas_call x0 -> x1, Pallas kernels: none -> 75.5 us  [shards(): pl.pallas_call(kernel, out_shape=jax.ShapeDtypeStruct((2, HALF), jnp.floa...]
    dot_general x1 -> x0, matrix products: 22.7 us -> none  [shards(): lax.dot_general(queries, piece_unit, (((1,), (1,)), ((), ())), preferred_...]
    all_gather x1 -> x0, blocking collectives: 19 us -> none  [shards(): piece_order = lax.all_gather(member_order, 'row', axis=0, tiled=True)]
    convert_element_type x1 -> x0, other arithmetic: 3.5 us -> none  [shards(): unit = (values * lax.rsqrt(squares + 1e-06)).astype(jnp.bfloat16)]
  transfers between devices with their start and end apart: 4 -> 0, of which waited for: 2 -> 0; matrix products, arithmetic and copies ran while one was open for 1% -> 0% of each run, Pallas kernels for 0% -> 0%
where the time goes in v1:
time: 80.4 us; the launch traced here: 80.2 us
  Pallas kernels  75.5 us (94%)
  local copies, waits for them, and re-layouts  3.4 us (4%)
  other arithmetic  1.33 us (2%)
    pallas_call x1, Pallas kernels, shards(): pl.pallas_call(kernel, out_shape=jax.ShapeDtypeStruct((2, HALF), jnp.floa...  75.5 us
    unnamed x3, local copies, waits for them, and re-layouts  2.16 us

profile of v1, /device:TPU:1, one launch (start us, length us, event | category | flops | bytes accessed | tf_op | source)
XLA Modules:
  0.0 80.2 jit_solution(10986135622952151784)
XLA Ops:
  0.0 1.2 %dynamic_slice.3 = s32[1]{0:T(128)} dynamic-slice(s32[4]{0:T(128)} %param.5, s32[]{:T(128)S(6)} %select_n.20), dynamic_slice_sizes={1} | dynamic-slice | bytes 12 | tf_op jit(solution)/shard_map/dynamic_slice | solution.py:263
  1.2 1.3 %fusion = s32[2,128]{1,0:T(2,128)S(1)} fusion(s32[256]{0:T(256)} %param.4, s32[]{:T(128)} %bitcast, s32[]{:T(128)S(6)} %add.18), kind=kLoop, calls=%fused_computation.1 | loop fusion | flops 768 | bytes 2056 | tf_op jit(solution)/shard_map/broadcast_in_dim | solution.py:265
  2.6 0.0 copy-start
  2.6 1.6 %copy-done = bf16[256,4096]{1,0:T(8,128)(2,1)S(1)} copy-done((bf16[256,4096]{1,0:T(8,128)(2,1)S(1)}, bf16[256,4096]{1,0:T(8,128)(2,1)}, u32[]{:S(2)}) %copy-start) | copy-done | bytes 2097176
  4.2 75.5 %nearest_earlier.1 = f32[2,128]{1,0:T(2,128)S(1)} custom-call(bf16[256,4096]{1,0:T(8,128)(2,1)S(1)} %copy-done, s32[2,8,128]{2,1,0:T(8,128)S(1)} %broadcast_in_dim.13.rank_ref), custom_call_target="tpu_custom_call" | custom-call | tf_op jit(solution)/shard_map/nearest_earlier/pallas_call | solution.py:268
  79.7 0.6 copy.5
  (1 shorter events, 0.0 us)
Async XLA Ops:
  2.6 1.6 %copy-start = (bf16[256,4096]{1,0:T(8,128)(2,1)S(1)}, bf16[256,4096]{1,0:T(8,128)(2,1)}, u32[]{:S(2)}) copy-start(bf16[256,4096]{1,0:T(8,128)(2,1)} %rows_hbm.1) | copy-start | bytes 6291460

commit v2 on v1

v2 whole, which is shorter than its diff:
```python
import jax
import jax.numpy as jnp
from jax import lax
from jax.experimental import pallas as pl
from jax.experimental.pallas import tpu as pltpu
from jax.sharding import PartitionSpec as P

MESH = pl.DeviceIdType.MESH
SIDE = 4
ROWS = 256
HALF = ROWS // 2
CHUNK = 64
CHUNKS = ROWS // CHUNK
ORDER = (2, 3, 0, 1)
EMPTY = 1 << 20
OTHER, NEAR, OTHER_LAST, FAR = 4, 7, 8, 9
SLOTS = 10
OTHERS = (OTHER, OTHER + 1, OTHER + 2, OTHER_LAST)
TURNED = 9 * HALF


def kernel(
    rows_hbm, order_hbm, count_hbm, out_ref, blocks, turned, turned_line, order, count, rank_lane, rank_row, best_row,
    best_lane, mail, load_sem, word_sem, send_sem, recv_sem, rank_send, rank_recv, mail_send, mail_recv,
):
    group, place = lax.axis_index("grp"), lax.axis_index("row")
    core = lax.rem(group, 2)
    x, y = place // SIDE, lax.rem(place, SIDE)

    def device(main, side, flip=False):
        dx = main * (1 - core) + side * core
        dy = main * core + side * (1 - core)
        there = lax.rem(x + dx + SIDE, SIDE) * SIDE + lax.rem(y + dy + SIDE, SIDE)
        return (group + 1 - 2 * core if flip else group, there)

    partner = device(0, 0, True)

    greeted = [device(i, 0) for i in (1, 2, 3)] + [device(0, i) for i in (1, 2, 3)]
    greeted += [partner] + [device(i, 0, True) for i in (1, 2, 3)] + [device(0, i, True) for i in (1, 2, 3)]
    barrier = pltpu.get_barrier_semaphore()
    for there in greeted:
        pl.semaphore_signal(barrier, inc=1, device_id=there, device_id_type=MESH)

    def load(c):
        at = pl.ds(c * CHUNK, CHUNK)
        return pltpu.make_async_copy(rows_hbm.at[at], blocks.at[0, at], load_sem.at[c])

    for c in ORDER:
        load(c).start()
    words = [
        pltpu.make_async_copy(order_hbm, order, word_sem.at[0]),
        pltpu.make_async_copy(count_hbm, count, word_sem.at[1]),
    ]
    for copy in words:
        copy.start()

    def normalise(c):
        load(c).wait()

        @pl.loop(0, CHUNK // 16)
        def _(i):
            at = pl.ds(pl.multiple_of(c * CHUNK + i * 16, 16), 16)
            values = blocks[0, at, :].astype(jnp.float32)
            squares = jnp.sum(values * values, axis=1, keepdims=True)
            blocks[0, at, :] = (values * lax.rsqrt(squares + 1e-06)).astype(jnp.bfloat16)

    def move(source, slot, c, there):
        at = pl.ds(c * CHUNK, CHUNK)
        return pltpu.make_async_remote_copy(
            blocks.at[source, at], blocks.at[slot, at], send_sem.at[slot, c], recv_sem.at[slot, c],
            device_id=there, device_id_type=MESH,
        )

    sent = []

    def send(source, slot, c, there):
        copy = move(source, slot, c, there)
        copy.start()
        sent.append(copy)

    def await_chunk(slot, c):
        move(slot, slot, c, partner).wait_recv()

    down, up, side_up = device(-1, 0), device(1, 0), device(0, 1)

    rank_to = [(i, device(-i, 0)) for i in (1, 2, 3)] + [(NEAR, side_up), (FAR, device(0, 2))]
    rank_to += [(OTHERS[i], device(-i, 0, True)) for i in range(4)]

    def pair(slot):
        return pl.ds(2 * slot, 2)

    def rank_copy(slot, there):
        return pltpu.make_async_remote_copy(
            rank_lane.at[pair(0)], rank_lane.at[pair(slot)], rank_send.at[slot], rank_recv.at[slot],
            device_id=there, device_id_type=MESH,
        )

    normalise(ORDER[0])
    for copy in words:
        copy.wait()
    slots = (core * SIDE * SIDE + place) * ROWS
    slots += lax.broadcasted_iota(jnp.int32, (2, HALF), 0) * HALF + lax.broadcasted_iota(jnp.int32, (2, HALF), 1)
    live = slots < count[group // 2]
    rank = jnp.where(live, order[...], EMPTY)
    rank_lane[pair(0)] = jnp.broadcast_to(rank[:, None, :], (2, 8, HALF))
    pl.semaphore_wait(barrier, len(greeted))
    for k, c in enumerate(ORDER):
        if k:
            normalise(c)
        send(0, 1, c, down)
        send(0, NEAR, c, side_up)
        if k >= CHUNKS // 2:
            send(0, 3, c, up)
        send(0, OTHER, c, partner)
        if k == 0:
            for slot, there in rank_to:
                rank_copy(slot, there).start()

    best_row[...] = jnp.full_like(best_row, -1.0)
    best_lane[...] = jnp.full_like(best_lane, -1.0)

    def column(slot):
        for h in range(2):
            wide = jnp.broadcast_to(rank_lane[2 * slot + h][:1], (HALF, HALF))
            rank_row[slot, pl.ds(h * HALF, HALF), :] = wide.T

    def turn(slot, into, first, rows=ROWS):
        @pl.loop(0, blocks.shape[2] // 256)
        def _(i):
            at = pl.ds(pl.multiple_of(i * 256, 256), 256)
            into[at, pl.ds(first, rows)] = blocks[slot, pl.ds(0, rows), at].T

    def reduce(scores, a, start, halves, both=True):
        rows = scores.shape[0]
        mine = rank_row[a, pl.ds(start, rows), :].reshape(rows // 8, 8, HALF)
        best = best_row[a, pl.ds(start, rows), :].reshape(rows // 8, 8, HALF)
        for i, half in enumerate(halves):
            part = scores[:, i * HALF : (i + 1) * HALF].reshape(rows // 8, 8, HALF)
            earlier = rank_lane[half][None] < mine
            best = jnp.maximum(best, jnp.where(earlier, part, -1.0))
            if both:
                best_lane[half] = jnp.maximum(best_lane[half], jnp.max(jnp.where(earlier, -1.0, part), axis=0))
        best_row[a, pl.ds(start, rows), :] = best.reshape(rows, HALF)

    def meet(a, b, start=0, rows=ROWS, other=0, other_rows=ROWS, both=True):
        left, right = blocks[a, pl.ds(start, rows), :], blocks[b, pl.ds(other, other_rows), :]
        scores = lax.dot_general(left, right, (((1,), (1,)), ((), ())), preferred_element_type=jnp.float32)
        first = 2 * b + other // HALF
        reduce(scores, a, start, [first + i for i in range(other_rows // HALF)], both)

    def meet_turned(a, start, rows, columns, first, count, half):
        scores = jnp.dot(
            blocks[a, pl.ds(start, rows), :], columns[:, pl.ds(first, count)], preferred_element_type=jnp.float32
        )
        reduce(scores, a, start, [half + i for i in range(count // HALF)])

    def meet_others(a, first, last):
        @pl.loop(first, last)
        def _(i):
            meet_turned(a, 0, ROWS, turned, pl.multiple_of(i * ROWS, ROWS), ROWS, 2 * OTHER + 2 * i)

    def fold(slot, halves=(0, 1)):
        for h in halves:
            flat = best_row[slot, pl.ds(h * HALF, HALF), :].T
            found = jnp.max(flat.reshape(HALF // 8, 8, HALF), axis=0)
            best_lane[2 * slot + h] = jnp.maximum(best_lane[2 * slot + h], found)

    def await_main(k):
        slot, c = 1 + k // CHUNKS, ORDER[k % CHUNKS]
        await_chunk(slot, c)
        if k < CHUNKS + CHUNKS // 2:
            send(slot, slot + 1, c, down)
        send(slot, OTHERS[slot], c, partner)

    def await_side(k):
        slot, c = (NEAR, FAR)[k // CHUNKS], ORDER[k % CHUNKS]
        await_chunk(slot, c)
        if k < CHUNKS:
            send(slot, FAR, c, side_up)

    def await_up(k):
        await_chunk(3, k)
        send(3, OTHER_LAST, k, partner)

    def await_other(slot, chunks=ORDER):
        for c in chunks:
            await_chunk(slot, c)

    column(0)
    meet(0, 0, both=False)
    turn(0, turned_line, 0)
    await_main(0)
    for slot, there in rank_to:
        rank_copy(slot, there).wait_recv()
    for slot in (1, 2, 3, FAR):
        column(slot)
    await_other(OTHER)
    turn(OTHER, turned, 0)
    meet_others(0, 0, 1)
    await_main(1)
    await_main(2)
    await_side(0)
    await_main(3)
    await_side(1)
    meet_turned(1, 0, ROWS, turned_line, 0, ROWS, 0)
    meet_others(1, 0, 1)
    turn(1, turned_line, ROWS)
    await_main(4)
    await_side(2)
    await_up(0)
    await_other(OTHER + 1)
    turn(OTHER + 1, turned, ROWS)
    meet_others(1, 1, 2)
    await_main(5)
    await_side(3)
    await_up(1)
    turn(NEAR, turned, 3 * ROWS)
    meet_others(0, 3, 4)
    meet_others(1, 3, 4)
    await_main(6)
    await_side(4)
    await_other(OTHER_LAST, ORDER[2:])
    turn(OTHER_LAST, turned, 4 * ROWS, HALF)
    await_main(7)
    await_side(5)
    meet_others(2, 0, 2)
    meet_others(2, 3, 4)
    meet_turned(2, 0, ROWS, turned_line, 0, ROWS, 0)
    turn(2, turned_line, 2 * ROWS)
    await_main(8)
    await_side(6)
    await_other(OTHER + 2)
    turn(OTHER + 2, turned, 2 * ROWS)
    meet_others(2, 2, 3)
    for slot in (0, 1, 2):
        fold(slot)

    owners = [(i, device(i, 0)) for i in (1, 2, 3)] + [(NEAR, device(0, -1)), (FAR, device(0, -2))]
    owners += [(OTHERS[i], device(0, i, True)) for i in range(4)]

    def mail_copy(slot, there):
        return pltpu.make_async_remote_copy(
            best_lane.at[pair(slot)], mail.at[pair(slot)], mail_send.at[slot], mail_recv.at[slot],
            device_id=there, device_id_type=MESH,
        )

    def post(*slots):
        for slot, there in owners:
            if slot in slots:
                mail_copy(slot, there).start()

    meet_turned(3, 0, HALF, turned, 0, TURNED, 2 * OTHER)
    meet_turned(FAR, HALF, HALF, turned_line, 0, 3 * ROWS, 0)
    fold(3, (0,))
    fold(FAR, (1,))
    await_main(9)
    await_side(7)
    meet_turned(3, HALF, HALF, turned, 0, TURNED, 2 * OTHER)
    post(OTHER, OTHER + 1, OTHER + 2, NEAR)
    meet_turned(FAR, 0, HALF, turned_line, 0, 3 * ROWS, 0)
    post(1, 2)
    fold(FAR, (0,))
    post(FAR)
    await_other(OTHER_LAST, ORDER[:2])
    meet(3, OTHER_LAST, HALF, HALF, HALF, HALF)
    post(OTHER_LAST)
    fold(3, (1,))
    post(3)

    found = best_lane[pair(0)]
    for slot, there in owners:
        mail_copy(slot, there).wait_recv()
        found = jnp.maximum(found, mail[pair(slot)])
    out_ref[...] = jnp.where(rank_lane[pair(0)][:, 0, :] < EMPTY, jnp.max(found, axis=1), -1.0)

    for copy in sent:
        copy.wait_send()
    for slot, there in rank_to:
        rank_copy(slot, there).wait_send()
    for slot, there in owners:
        mail_copy(slot, there).wait_send()


def shards(embeddings, member_order, member_count):
    rows, depth = embeddings.shape
    copies = [pltpu.SemaphoreType.DMA((SLOTS, CHUNKS))] * 2
    letters = [pltpu.SemaphoreType.DMA((SLOTS,))] * 4
    best = pl.pallas_call(
        kernel,
        out_shape=jax.ShapeDtypeStruct((2, HALF), jnp.float32),
        in_specs=[pl.BlockSpec(memory_space=pltpu.HBM)] * 3,
        out_specs=pl.BlockSpec(memory_space=pltpu.VMEM),
        scratch_shapes=[
            pltpu.VMEM((SLOTS, rows, depth), jnp.bfloat16),
            pltpu.VMEM((depth, TURNED), jnp.bfloat16),
            pltpu.VMEM((depth, 3 * rows), jnp.bfloat16),
            pltpu.VMEM((2, HALF), jnp.int32),
            pltpu.SMEM(member_count.shape, jnp.int32),
            pltpu.VMEM((2 * SLOTS, 8, HALF), jnp.int32),
            pltpu.VMEM((SLOTS, rows, HALF), jnp.int32),
            pltpu.VMEM((SLOTS, rows, HALF), jnp.float32),
            pltpu.VMEM((2 * SLOTS, 8, HALF), jnp.float32),
            pltpu.VMEM((2 * SLOTS, 8, HALF), jnp.float32),
            pltpu.SemaphoreType.DMA((CHUNKS,)),
            pltpu.SemaphoreType.DMA((2,)),
            *copies,
            *letters,
        ],
        compiler_params=pltpu.CompilerParams(collective_id=0, has_side_effects=True, vmem_limit_bytes=60 * 2**20),
        name="nearest_earlier",
    )(embeddings, member_order.reshape(2, HALF), member_count)
    return best.reshape(rows)


def solution(mesh):
    in_specs = (P(("grp", "row"), None), P(("grp", "row")), P())
    out_specs = P(("grp", "row"))
    return jax.shard_map(shards, mesh=mesh, in_specs=in_specs, out_specs=out_specs, check_vma=False)
```

time: 80.4 us -> 73.7 us (0.917)
  Pallas kernels: 75.5 us -> 72 us
  local copies, waits for them, and re-layouts: 3.4 us -> 1.24 us
  other arithmetic: 1.33 us -> 0 us
    pallas_call x1, Pallas kernels: 75.5 us -> 72 us  [shards(): pl.pallas_call(kernel, out_shape=jax.ShapeDtypeStruct((2, HALF), jnp.floa...]
    broadcast_in_dim x1 -> x0, other arithmetic: 1.33 us -> none  [shards(): rank = jnp.broadcast_to(rank, (2, 8, HALF))]
    dynamic_slice x1 -> x0, local copies, waits for them, and re-layouts: 1.24 us -> none  [shards(): live = base + jnp.arange(rows, dtype=jnp.int32) < member_count[group // 2]]
    unnamed x3 -> x1, local copies, waits for them, and re-layouts: 2.16 us -> 1.24 us
where the time goes in v2:
time: 73.7 us; the launch traced here: 73.3 us
  Pallas kernels  72 us (98%)
  local copies, waits for them, and re-layouts  1.24 us (2%)
    pallas_call x1, Pallas kernels, shards(): pl.pallas_call(kernel, out_shape=jax.ShapeDtypeStruct((2, HALF), jnp.floa...  72 us

profile of v2, /device:TPU:1, one launch (start us, length us, event | category | flops | bytes accessed | tf_op | source)
XLA Modules:
  0.0 73.3 jit_solution(10640548002388229078)
XLA Ops:
  0.0 72.0 %nearest_earlier.1 = f32[2,128]{1,0:T(2,128)} custom-call(bf16[256,4096]{1,0:T(8,128)(2,1)} %rows_hbm.1, s32[2,128]{1,0:T(2,128)} %bitcast.3, s32[4]{0:T(128)} %count_hbm.1), custom_call_target="tpu_custom_call" | custom-call | tf_op jit(solution)/shard_map/nearest_earlier/pallas_call | solution.py:288
  72.0 1.2 %copy.5 = f32[256]{0:T(256)} copy(f32[256]{0:T(256)} %bitcast.2) | data formatting | bytes 2048

commit v3 on v2

--- a/solution.py
+++ b/solution.py
@@ -13,14 +13,14 @@
 CHUNKS = ROWS // CHUNK
 ORDER = (2, 3, 0, 1)
 EMPTY = 1 << 20
-OTHER, NEAR, OTHER_LAST, FAR = 4, 7, 8, 9
-SLOTS = 10
+OTHER, NEAR, OTHER_LAST, FAR, RELAY = 4, 7, 8, 9, 10
+SLOTS = 11
 OTHERS = (OTHER, OTHER + 1, OTHER + 2, OTHER_LAST)
-TURNED = 9 * HALF
+TURNED = 4 * ROWS
 
 
 def kernel(
-    rows_hbm, order_hbm, count_hbm, out_ref, blocks, turned, turned_line, order, count, rank_lane, rank_row, best_row,
+    rows_hbm, order_hbm, count_hbm, out_ref, blocks, turned, turned_own, order, count, rank_lane, rank_row, best_row,
     best_lane, mail, load_sem, word_sem, send_sem, recv_sem, rank_send, rank_recv, mail_send, mail_recv,
 ):
     group, place = lax.axis_index("grp"), lax.axis_index("row")
@@ -34,9 +34,15 @@
         return (group + 1 - 2 * core if flip else group, there)
 
     partner = device(0, 0, True)
+    parity = lax.rem(group // 2, 2)
+    step = 1 - 2 * lax.rem(parity + core, 2)
+    across = (lax.rem(group // 2 + step + SIDE, SIDE) * 2 + core, place)
+    along = x * core + y * (1 - core)
+    near_goes_on = lax.rem(along + 3, SIDE) // 2 == parity
+    far_here = lax.rem(along + 2, SIDE) // 2 == parity
 
     greeted = [device(i, 0) for i in (1, 2, 3)] + [device(0, i) for i in (1, 2, 3)]
-    greeted += [partner] + [device(i, 0, True) for i in (1, 2, 3)] + [device(0, i, True) for i in (1, 2, 3)]
+    greeted += [partner, across] + [device(i, 0, True) for i in (1, 2, 3)] + [device(0, i, True) for i in (1, 2, 3)]
     barrier = pltpu.get_barrier_semaphore()
     for there in greeted:
         pl.semaphore_signal(barrier, inc=1, device_id=there, device_id_type=MESH)
@@ -64,10 +70,10 @@
             squares = jnp.sum(values * values, axis=1, keepdims=True)
             blocks[0, at, :] = (values * lax.rsqrt(squares + 1e-06)).astype(jnp.bfloat16)
 
-    def move(source, slot, c, there):
+    def move(source, slot, c, there, leaves=None):
         at = pl.ds(c * CHUNK, CHUNK)
         return pltpu.make_async_remote_copy(
-            blocks.at[source, at], blocks.at[slot, at], send_sem.at[slot, c], recv_sem.at[slot, c],
+            blocks.at[source, at], blocks.at[slot, at], leaves or send_sem.at[slot, c], recv_sem.at[slot, c],
             device_id=there, device_id_type=MESH,
         )
 
@@ -77,6 +83,18 @@
         copy = move(source, slot, c, there)
         copy.start()
         sent.append(copy)
+
+    def direct(c):
+        return move(NEAR, FAR, c, side_up)
+
+    def out(c):
+        return move(NEAR, RELAY, c, across)
+
+    def relayed(c):
+        return move(RELAY, FAR, c, side_up)
+
+    def back(c):
+        return move(FAR, FAR, c, across, send_sem.at[RELAY, c - CHUNKS // 2])
 
     def await_chunk(slot, c):
         move(slot, slot, c, partner).wait_recv()
@@ -109,8 +127,6 @@
             normalise(c)
         send(0, 1, c, down)
         send(0, NEAR, c, side_up)
-        if k >= CHUNKS // 2:
-            send(0, 3, c, up)
         send(0, OTHER, c, partner)
         if k == 0:
             for slot, there in rank_to:
@@ -124,11 +140,11 @@
             wide = jnp.broadcast_to(rank_lane[2 * slot + h][:1], (HALF, HALF))
             rank_row[slot, pl.ds(h * HALF, HALF), :] = wide.T
 
-    def turn(slot, into, first, rows=ROWS):
+    def turn(slot, into, first, start=0, rows=ROWS):
         @pl.loop(0, blocks.shape[2] // 256)
         def _(i):
             at = pl.ds(pl.multiple_of(i * 256, 256), 256)
-            into[at, pl.ds(first, rows)] = blocks[slot, pl.ds(0, rows), at].T
+            into[at, pl.ds(first, rows)] = blocks[slot, pl.ds(start, rows), at].T
 
     def reduce(scores, a, start, halves, both=True):
         rows = scores.shape[0]
@@ -168,15 +184,36 @@
     def await_main(k):
         slot, c = 1 + k // CHUNKS, ORDER[k % CHUNKS]
         await_chunk(slot, c)
-        if k < CHUNKS + CHUNKS // 2:
+        if k <= CHUNKS:
             send(slot, slot + 1, c, down)
         send(slot, OTHERS[slot], c, partner)
-
-    def await_side(k):
-        slot, c = (NEAR, FAR)[k // CHUNKS], ORDER[k % CHUNKS]
-        await_chunk(slot, c)
-        if k < CHUNKS:
-            send(slot, FAR, c, side_up)
+        if k == 5:
+            for c in ORDER[2:] + ORDER[1:2]:
+                send(0, 3, c, up)
+
+    def await_near(c):
+        await_chunk(NEAR, c)
+
+        @pl.when(near_goes_on)
+        def _():
+            (direct if c in ORDER[2:] else out)(c).start()
+
+    def await_relay(c):
+        @pl.when(jnp.logical_not(near_goes_on))
+        def _():
+            await_chunk(RELAY, c)
+            relayed(c).start()
+
+    def await_far(c):
+        @pl.when(far_here)
+        def _():
+            await_chunk(FAR, c)
+
+    def await_back(c):
+        @pl.when(jnp.logical_not(far_here))
+        def _():
+            await_chunk(FAR, c)
+            back(c).start()
 
     def await_up(k):
         await_chunk(3, k)
@@ -188,50 +225,61 @@
 
     column(0)
     meet(0, 0, both=False)
-    turn(0, turned_line, 0)
+    turn(0, turned_own, 0)
     await_main(0)
+    await_near(ORDER[0])
     for slot, there in rank_to:
         rank_copy(slot, there).wait_recv()
-    for slot in (1, 2, 3, FAR):
+    for slot in (1, 2, 3):
         column(slot)
     await_other(OTHER)
     turn(OTHER, turned, 0)
     meet_others(0, 0, 1)
     await_main(1)
+    await_near(ORDER[1])
+    await_relay(ORDER[0])
     await_main(2)
-    await_side(0)
+    await_near(ORDER[2])
+    await_relay(ORDER[1])
     await_main(3)
-    await_side(1)
-    meet_turned(1, 0, ROWS, turned_line, 0, ROWS, 0)
+    await_near(ORDER[3])
+    meet_turned(1, 0, ROWS, turned_own, 0, ROWS, 0)
     meet_others(1, 0, 1)
-    turn(1, turned_line, ROWS)
     await_main(4)
-    await_side(2)
-    await_up(0)
+    await_back(ORDER[0])
     await_other(OTHER + 1)
     turn(OTHER + 1, turned, ROWS)
     meet_others(1, 1, 2)
+    turn(NEAR, turned, 3 * ROWS)
     await_main(5)
-    await_side(3)
-    await_up(1)
-    turn(NEAR, turned, 3 * ROWS)
+    await_back(ORDER[1])
     meet_others(0, 3, 4)
     meet_others(1, 3, 4)
+    meet_turned(2, HALF, HALF, turned_own, 0, ROWS, 0)
+    meet_turned(2, HALF, HALF, turned, 0, 2 * ROWS, 2 * OTHER)
+    meet_turned(2, HALF, HALF, turned, 3 * ROWS, ROWS, 2 * NEAR)
     await_main(6)
-    await_side(4)
-    await_other(OTHER_LAST, ORDER[2:])
-    turn(OTHER_LAST, turned, 4 * ROWS, HALF)
+    await_up(ORDER[2])
+    await_other(OTHER + 2, ORDER[:2])
+    turn(OTHER + 2, turned, 2 * ROWS + HALF, HALF, HALF)
     await_main(7)
-    await_side(5)
-    meet_others(2, 0, 2)
-    meet_others(2, 3, 4)
-    meet_turned(2, 0, ROWS, turned_line, 0, ROWS, 0)
-    turn(2, turned_line, 2 * ROWS)
-    await_main(8)
-    await_side(6)
-    await_other(OTHER + 2)
-    turn(OTHER + 2, turned, 2 * ROWS)
+    meet_turned(2, 0, HALF, turned_own, 0, HALF, 0)
+    meet_turned(2, 0, HALF, turned, 0, 2 * ROWS, 2 * OTHER)
+    meet_turned(2, 0, HALF, turned, 3 * ROWS, ROWS, 2 * NEAR)
+    await_other(OTHER + 2, ORDER[2:])
+    turn(OTHER + 2, turned, 2 * ROWS, 0, HALF)
     meet_others(2, 2, 3)
+    await_up(ORDER[3])
+    meet_turned(3, 0, HALF, turned, 0, TURNED, 2 * OTHER)
+    for c in ORDER:
+        await_far(c)
+
+    @pl.when(far_here)
+    def _():
+        @pl.loop(0, 3)
+        def _(a):
+            meet(a, FAR)
+
     for slot in (0, 1, 2):
         fold(slot)
 
@@ -249,22 +297,21 @@
             if slot in slots:
                 mail_copy(slot, there).start()
 
-    meet_turned(3, 0, HALF, turned, 0, TURNED, 2 * OTHER)
-    meet_turned(FAR, HALF, HALF, turned_line, 0, 3 * ROWS, 0)
-    fold(3, (0,))
-    fold(FAR, (1,))
-    await_main(9)
-    await_side(7)
+    post(1, 2)
+    await_main(8)
+    await_up(ORDER[1])
     meet_turned(3, HALF, HALF, turned, 0, TURNED, 2 * OTHER)
     post(OTHER, OTHER + 1, OTHER + 2, NEAR)
-    meet_turned(FAR, 0, HALF, turned_line, 0, 3 * ROWS, 0)
-    post(1, 2)
-    fold(FAR, (0,))
+
+    @pl.when(far_here)
+    def _():
+        meet(3, FAR)
+
     post(FAR)
-    await_other(OTHER_LAST, ORDER[:2])
-    meet(3, OTHER_LAST, HALF, HALF, HALF, HALF)
+    await_other(OTHER_LAST)
+    meet(3, OTHER_LAST)
     post(OTHER_LAST)
-    fold(3, (1,))
+    fold(3)
     post(3)
 
     found = best_lane[pair(0)]
@@ -275,6 +322,24 @@
 
     for copy in sent:
         copy.wait_send()
+
+    @pl.when(near_goes_on)
+    def _():
+        for c in ORDER[:2]:
+            out(c).wait_send()
+        for c in ORDER[2:]:
+            direct(c).wait_send()
+
+    @pl.when(jnp.logical_not(near_goes_on))
+    def _():
+        for c in ORDER[:2]:
+            relayed(c).wait_send()
+
+    @pl.when(jnp.logical_not(far_here))
+    def _():
+        for c in ORDER[:2]:
+            back(c).wait_send()
+
     for slot, there in rank_to:
         rank_copy(slot, there).wait_send()
     for slot, there in owners:
@@ -293,7 +358,7 @@
         scratch_shapes=[
             pltpu.VMEM((SLOTS, rows, depth), jnp.bfloat16),
             pltpu.VMEM((depth, TURNED), jnp.bfloat16),
-            pltpu.VMEM((depth, 3 * rows), jnp.bfloat16),
+            pltpu.VMEM((depth, rows), jnp.bfloat16),
             pltpu.VMEM((2, HALF), jnp.int32),
             pltpu.SMEM(member_count.shape, jnp.int32),
             pltpu.VMEM((2 * SLOTS, 8, HALF), jnp.int32),

time: 73.7 us -> 70.7 us (0.959)
  Pallas kernels: 72 us -> 69.3 us
    pallas_call x1, Pallas kernels: 72 us -> 69.3 us  [shards(): pl.pallas_call(kernel, out_shape=jax.ShapeDtypeStruct((2, HALF), jnp.floa...]
where the time goes in v3:
time: 70.7 us; the launch traced here: 70.5 us
  Pallas kernels  69.3 us (98%)
  local copies, waits for them, and re-layouts  1.24 us (2%)
    pallas_call x1, Pallas kernels, shards(): pl.pallas_call(kernel, out_shape=jax.ShapeDtypeStruct((2, HALF), jnp.floa...  69.3 us

profile of v3, /device:TPU:1, one launch (start us, length us, event | category | flops | bytes accessed | tf_op | source)
XLA Modules:
  0.0 70.5 jit_solution(13124264342533460641)
XLA Ops:
  0.0 69.3 %nearest_earlier.1 = f32[2,128]{1,0:T(2,128)} custom-call(bf16[256,4096]{1,0:T(8,128)(2,1)} %rows_hbm.1, s32[2,128]{1,0:T(2,128)} %bitcast.3, s32[4]{0:T(128)} %count_hbm.1), custom_call_target="tpu_custom_call" | custom-call | tf_op jit(solution)/shard_map/nearest_earlier/pallas_call | solution.py:353
  69.3 1.2 %copy.5 = f32[256]{0:T(256)} copy(f32[256]{0:T(256)} %bitcast.2) | data formatting | bytes 2048

commit v4 on v3

--- a/solution.py
+++ b/solution.py
@@ -36,16 +36,11 @@
     partner = device(0, 0, True)
     parity = lax.rem(group // 2, 2)
     step = 1 - 2 * lax.rem(parity + core, 2)
-    across = (lax.rem(group // 2 + step + SIDE, SIDE) * 2 + core, place)
+    plane = lax.rem(group // 2 + step + SIDE, SIDE) * 2 + core
+    across, ahead, behind = (plane, place), (plane, device(0, 1)[1]), (plane, device(0, -1)[1])
     along = x * core + y * (1 - core)
     near_goes_on = lax.rem(along + 3, SIDE) // 2 == parity
     far_here = lax.rem(along + 2, SIDE) // 2 == parity
-
-    greeted = [device(i, 0) for i in (1, 2, 3)] + [device(0, i) for i in (1, 2, 3)]
-    greeted += [partner, across] + [device(i, 0, True) for i in (1, 2, 3)] + [device(0, i, True) for i in (1, 2, 3)]
-    barrier = pltpu.get_barrier_semaphore()
-    for there in greeted:
-        pl.semaphore_signal(barrier, inc=1, device_id=there, device_id_type=MESH)
 
     def load(c):
         at = pl.ds(c * CHUNK, CHUNK)
@@ -60,6 +55,12 @@
     for copy in words:
         copy.start()
 
+    greeted = [device(i, 0) for i in (1, 2, 3)] + [device(0, i) for i in (1, 2, 3)]
+    greeted += [partner, across, ahead, behind] + [device(i, 0, True) for i in (1, 2, 3)] + [device(0, i, True) for i in (1, 2, 3)]
+    barrier = pltpu.get_barrier_semaphore()
+    for there in greeted:
+        pl.semaphore_signal(barrier, inc=1, device_id=there, device_id_type=MESH)
+
     def normalise(c):
         load(c).wait()
 
@@ -70,10 +71,10 @@
             squares = jnp.sum(values * values, axis=1, keepdims=True)
             blocks[0, at, :] = (values * lax.rsqrt(squares + 1e-06)).astype(jnp.bfloat16)
 
-    def move(source, slot, c, there, leaves=None):
+    def move(source, slot, c, there):
         at = pl.ds(c * CHUNK, CHUNK)
         return pltpu.make_async_remote_copy(
-            blocks.at[source, at], blocks.at[slot, at], leaves or send_sem.at[slot, c], recv_sem.at[slot, c],
+            blocks.at[source, at], blocks.at[slot, at], send_sem.at[slot, c], recv_sem.at[slot, c],
             device_id=there, device_id_type=MESH,
         )
 
@@ -91,10 +92,7 @@
         return move(NEAR, RELAY, c, across)
 
     def relayed(c):
-        return move(RELAY, FAR, c, side_up)
-
-    def back(c):
-        return move(FAR, FAR, c, across, send_sem.at[RELAY, c - CHUNKS // 2])
+        return move(RELAY, FAR, c, ahead)
 
     def await_chunk(slot, c):
         move(slot, slot, c, partner).wait_recv()
@@ -187,7 +185,7 @@
         if k <= CHUNKS:
             send(slot, slot + 1, c, down)
         send(slot, OTHERS[slot], c, partner)
-        if k == 5:
+        if k == 4:
             for c in ORDER[2:] + ORDER[1:2]:
                 send(0, 3, c, up)
 
@@ -208,12 +206,6 @@
         @pl.when(far_here)
         def _():
             await_chunk(FAR, c)
-
-    def await_back(c):
-        @pl.when(jnp.logical_not(far_here))
-        def _():
-            await_chunk(FAR, c)
-            back(c).start()
 
     def await_up(k):
         await_chunk(3, k)
@@ -246,13 +238,11 @@
     meet_turned(1, 0, ROWS, turned_own, 0, ROWS, 0)
     meet_others(1, 0, 1)
     await_main(4)
-    await_back(ORDER[0])
     await_other(OTHER + 1)
     turn(OTHER + 1, turned, ROWS)
     meet_others(1, 1, 2)
     turn(NEAR, turned, 3 * ROWS)
     await_main(5)
-    await_back(ORDER[1])
     meet_others(0, 3, 4)
     meet_others(1, 3, 4)
     meet_turned(2, HALF, HALF, turned_own, 0, ROWS, 0)
@@ -262,6 +252,15 @@
     await_up(ORDER[2])
     await_other(OTHER + 2, ORDER[:2])
     turn(OTHER + 2, turned, 2 * ROWS + HALF, HALF, HALF)
+    for c in ORDER:
+        await_far(c)
+
+    @pl.when(far_here)
+    def _():
+        @pl.loop(0, 2)
+        def _(a):
+            meet(a, FAR)
+
     await_main(7)
     meet_turned(2, 0, HALF, turned_own, 0, HALF, 0)
     meet_turned(2, 0, HALF, turned, 0, 2 * ROWS, 2 * OTHER)
@@ -270,16 +269,12 @@
     turn(OTHER + 2, turned, 2 * ROWS, 0, HALF)
     meet_others(2, 2, 3)
     await_up(ORDER[3])
+
+    @pl.when(far_here)
+    def _():
+        meet(2, FAR)
+
     meet_turned(3, 0, HALF, turned, 0, TURNED, 2 * OTHER)
-    for c in ORDER:
-        await_far(c)
-
-    @pl.when(far_here)
-    def _():
-        @pl.loop(0, 3)
-        def _(a):
-            meet(a, FAR)
-
     for slot in (0, 1, 2):
         fold(slot)
 
@@ -308,11 +303,32 @@
         meet(3, FAR)
 
     post(FAR)
-    await_other(OTHER_LAST)
-    meet(3, OTHER_LAST)
+    await_other(OTHER_LAST, ORDER[2:])
+    meet(3, OTHER_LAST, other_rows=HALF)
+    fold(3, (0,))
+    await_other(OTHER_LAST, ORDER[:2])
+    meet(3, OTHER_LAST, HALF, HALF, HALF, HALF)
     post(OTHER_LAST)
-    fold(3)
+    fold(3, (1,))
     post(3)
+
+    for copy in sent:
+        copy.wait_send()
+
+    @pl.when(near_goes_on)
+    def _():
+        for c in ORDER[:2]:
+            out(c).wait_send()
+        for c in ORDER[2:]:
+            direct(c).wait_send()
+
+    @pl.when(jnp.logical_not(near_goes_on))
+    def _():
+        for c in ORDER[:2]:
+            relayed(c).wait_send()
+
+    for slot, there in rank_to:
+        rank_copy(slot, there).wait_send()
 
     found = best_lane[pair(0)]
     for slot, there in owners:
@@ -320,28 +336,6 @@
         found = jnp.maximum(found, mail[pair(slot)])
     out_ref[...] = jnp.where(rank_lane[pair(0)][:, 0, :] < EMPTY, jnp.max(found, axis=1), -1.0)
 
-    for copy in sent:
-        copy.wait_send()
-
-    @pl.when(near_goes_on)
-    def _():
-        for c in ORDER[:2]:
-            out(c).wait_send()
-        for c in ORDER[2:]:
-            direct(c).wait_send()
-
-    @pl.when(jnp.logical_not(near_goes_on))
-    def _():
-        for c in ORDER[:2]:
-            relayed(c).wait_send()
-
-    @pl.when(jnp.logical_not(far_here))
-    def _():
-        for c in ORDER[:2]:
-            back(c).wait_send()
-
-    for slot, there in rank_to:
-        rank_copy(slot, there).wait_send()
     for slot, there in owners:
         mail_copy(slot, there).wait_send()
 

time: 70.7 us -> 69.4 us (0.982)
  Pallas kernels: 69.3 us -> 68 us
    pallas_call x1, Pallas kernels: 69.3 us -> 68 us  [shards(): pl.pallas_call(kernel, out_shape=jax.ShapeDtypeStruct((2, HALF), jnp.floa...]
where the time goes in v4:
time: 69.4 us; the launch traced here: 69.3 us
  Pallas kernels  68 us (98%)
  local copies, waits for them, and re-layouts  1.24 us (2%)
    pallas_call x1, Pallas kernels, shards(): pl.pallas_call(kernel, out_shape=jax.ShapeDtypeStruct((2, HALF), jnp.floa...  68 us

profile of v4, /device:TPU:1, one launch (start us, length us, event | category | flops | bytes accessed | tf_op | source)
XLA Modules:
  0.0 69.3 jit_solution(3746778515866370428)
XLA Ops:
  0.0 68.0 %nearest_earlier.1 = f32[2,128]{1,0:T(2,128)} custom-call(bf16[256,4096]{1,0:T(8,128)(2,1)} %rows_hbm.1, s32[2,128]{1,0:T(2,128)} %bitcast.3, s32[4]{0:T(128)} %count_hbm.1), custom_call_target="tpu_custom_call" | custom-call | tf_op jit(solution)/shard_map/nearest_earlier/pallas_call | solution.py:347
  68.1 1.2 %copy.5 = f32[256]{0:T(256)} copy(f32[256]{0:T(256)} %bitcast.2) | data formatting | bytes 2048

commit v5 on v4

--- a/solution.py
+++ b/solution.py
@@ -21,7 +21,7 @@
 
 def kernel(
     rows_hbm, order_hbm, count_hbm, out_ref, blocks, turned, turned_own, order, count, rank_lane, rank_row, best_row,
-    best_lane, mail, load_sem, word_sem, send_sem, recv_sem, rank_send, rank_recv, mail_send, mail_recv,
+    best_lane, mail, load_sem, word_sem, recv_sem, send_sem, branch_sem, rank_send, rank_recv, mail_send, mail_recv,
 ):
     group, place = lax.axis_index("grp"), lax.axis_index("row")
     core = lax.rem(group, 2)
@@ -71,31 +71,41 @@
             squares = jnp.sum(values * values, axis=1, keepdims=True)
             blocks[0, at, :] = (values * lax.rsqrt(squares + 1e-06)).astype(jnp.bfloat16)
 
-    def move(source, slot, c, there):
-        at = pl.ds(c * CHUNK, CHUNK)
+    def arrival(slot, c):
+        late = int(c < CHUNKS // 2)
+        if slot < OTHER:
+            index = (slot - 1) * CHUNKS + c
+        elif slot == NEAR:
+            index = 12 + c
+        elif slot == RELAY:
+            index = 16 + c - CHUNKS // 2
+        else:
+            index = {OTHER: 18, OTHER + 1: 19, OTHER + 2: 20 + late, OTHER_LAST: 22 + late, FAR: 24}[slot]
+        return recv_sem.at[index]
+
+    def move(source, slot, c, there, leaves=send_sem, chunks=1):
+        at = pl.ds(c * CHUNK, chunks * CHUNK)
         return pltpu.make_async_remote_copy(
-            blocks.at[source, at], blocks.at[slot, at], send_sem.at[slot, c], recv_sem.at[slot, c],
-            device_id=there, device_id_type=MESH,
+            blocks.at[source, at], blocks.at[slot, at], leaves, arrival(slot, c), device_id=there, device_id_type=MESH
         )
 
     sent = []
 
     def send(source, slot, c, there):
-        copy = move(source, slot, c, there)
-        copy.start()
-        sent.append(copy)
+        move(source, slot, c, there).start()
+        sent.append(slot)
 
     def direct(c):
-        return move(NEAR, FAR, c, side_up)
+        return move(NEAR, FAR, c, side_up, branch_sem)
 
     def out(c):
-        return move(NEAR, RELAY, c, across)
+        return move(NEAR, RELAY, c, across, branch_sem)
 
     def relayed(c):
-        return move(RELAY, FAR, c, ahead)
-
-    def await_chunk(slot, c):
-        move(slot, slot, c, partner).wait_recv()
+        return move(RELAY, FAR, c, ahead, branch_sem)
+
+    def await_chunk(slot, c, chunks=1):
+        move(slot, slot, c, partner, chunks=chunks).wait_recv()
 
     down, up, side_up = device(-1, 0), device(1, 0), device(0, 1)
 
@@ -107,7 +117,7 @@
 
     def rank_copy(slot, there):
         return pltpu.make_async_remote_copy(
-            rank_lane.at[pair(0)], rank_lane.at[pair(slot)], rank_send.at[slot], rank_recv.at[slot],
+            rank_lane.at[pair(0)], rank_lane.at[pair(slot)], rank_send, rank_recv,
             device_id=there, device_id_type=MESH,
         )
 
@@ -202,29 +212,23 @@
             await_chunk(RELAY, c)
             relayed(c).start()
 
-    def await_far(c):
-        @pl.when(far_here)
-        def _():
-            await_chunk(FAR, c)
-
     def await_up(k):
         await_chunk(3, k)
         send(3, OTHER_LAST, k, partner)
-
-    def await_other(slot, chunks=ORDER):
-        for c in chunks:
-            await_chunk(slot, c)
 
     column(0)
     meet(0, 0, both=False)
     turn(0, turned_own, 0)
     await_main(0)
     await_near(ORDER[0])
-    for slot, there in rank_to:
-        rank_copy(slot, there).wait_recv()
+    letters = pl.ds(2, 2 * len(rank_to))
+    ranks = pltpu.make_async_remote_copy(
+        rank_lane.at[letters], rank_lane.at[letters], rank_send, rank_recv, device_id=partner, device_id_type=MESH
+    )
+    ranks.wait_recv()
     for slot in (1, 2, 3):
         column(slot)
-    await_other(OTHER)
+    await_chunk(OTHER, 0, CHUNKS)
     turn(OTHER, turned, 0)
     meet_others(0, 0, 1)
     await_main(1)
@@ -238,7 +242,7 @@
     meet_turned(1, 0, ROWS, turned_own, 0, ROWS, 0)
     meet_others(1, 0, 1)
     await_main(4)
-    await_other(OTHER + 1)
+    await_chunk(OTHER + 1, 0, CHUNKS)
     turn(OTHER + 1, turned, ROWS)
     meet_others(1, 1, 2)
     turn(NEAR, turned, 3 * ROWS)
@@ -250,13 +254,13 @@
     meet_turned(2, HALF, HALF, turned, 3 * ROWS, ROWS, 2 * NEAR)
     await_main(6)
     await_up(ORDER[2])
-    await_other(OTHER + 2, ORDER[:2])
+    await_chunk(OTHER + 2, CHUNKS // 2, CHUNKS // 2)
     turn(OTHER + 2, turned, 2 * ROWS + HALF, HALF, HALF)
-    for c in ORDER:
-        await_far(c)
 
     @pl.when(far_here)
     def _():
+        await_chunk(FAR, 0, CHUNKS)
+
         @pl.loop(0, 2)
         def _(a):
             meet(a, FAR)
@@ -265,7 +269,7 @@
     meet_turned(2, 0, HALF, turned_own, 0, HALF, 0)
     meet_turned(2, 0, HALF, turned, 0, 2 * ROWS, 2 * OTHER)
     meet_turned(2, 0, HALF, turned, 3 * ROWS, ROWS, 2 * NEAR)
-    await_other(OTHER + 2, ORDER[2:])
+    await_chunk(OTHER + 2, 0, CHUNKS // 2)
     turn(OTHER + 2, turned, 2 * ROWS, 0, HALF)
     meet_others(2, 2, 3)
     await_up(ORDER[3])
@@ -283,7 +287,7 @@
 
     def mail_copy(slot, there):
         return pltpu.make_async_remote_copy(
-            best_lane.at[pair(slot)], mail.at[pair(slot)], mail_send.at[slot], mail_recv.at[slot],
+            best_lane.at[pair(slot)], mail.at[pair(slot)], mail_send, mail_recv,
             device_id=there, device_id_type=MESH,
         )
 
@@ -303,47 +307,41 @@
         meet(3, FAR)
 
     post(FAR)
-    await_other(OTHER_LAST, ORDER[2:])
+    await_chunk(OTHER_LAST, 0, CHUNKS // 2)
     meet(3, OTHER_LAST, other_rows=HALF)
     fold(3, (0,))
-    await_other(OTHER_LAST, ORDER[:2])
+    await_chunk(OTHER_LAST, CHUNKS // 2, CHUNKS // 2)
     meet(3, OTHER_LAST, HALF, HALF, HALF, HALF)
     post(OTHER_LAST)
     fold(3, (1,))
     post(3)
 
-    for copy in sent:
-        copy.wait_send()
+    whole = pl.ds(0, len(sent) // CHUNKS)
+    pltpu.make_async_copy(blocks.at[whole], blocks.at[whole], send_sem).wait()
 
     @pl.when(near_goes_on)
     def _():
-        for c in ORDER[:2]:
-            out(c).wait_send()
-        for c in ORDER[2:]:
-            direct(c).wait_send()
+        pltpu.make_async_copy(blocks.at[0], blocks.at[0], branch_sem).wait()
 
     @pl.when(jnp.logical_not(near_goes_on))
     def _():
-        for c in ORDER[:2]:
-            relayed(c).wait_send()
-
-    for slot, there in rank_to:
-        rank_copy(slot, there).wait_send()
-
+        half = blocks.at[0, pl.ds(0, HALF)]
+        pltpu.make_async_copy(half, half, branch_sem).wait()
+
+    ranks.wait_send()
+    mails = pltpu.make_async_remote_copy(
+        best_lane.at[letters], mail.at[letters], mail_send, mail_recv, device_id=partner, device_id_type=MESH
+    )
+    mails.wait_recv()
     found = best_lane[pair(0)]
     for slot, there in owners:
-        mail_copy(slot, there).wait_recv()
         found = jnp.maximum(found, mail[pair(slot)])
     out_ref[...] = jnp.where(rank_lane[pair(0)][:, 0, :] < EMPTY, jnp.max(found, axis=1), -1.0)
-
-    for slot, there in owners:
-        mail_copy(slot, there).wait_send()
+    mails.wait_send()
 
 
 def shards(embeddings, member_order, member_count):
     rows, depth = embeddings.shape
-    copies = [pltpu.SemaphoreType.DMA((SLOTS, CHUNKS))] * 2
-    letters = [pltpu.SemaphoreType.DMA((SLOTS,))] * 4
     best = pl.pallas_call(
         kernel,
         out_shape=jax.ShapeDtypeStruct((2, HALF), jnp.float32),
@@ -362,8 +360,8 @@
             pltpu.VMEM((2 * SLOTS, 8, HALF), jnp.float32),
             pltpu.SemaphoreType.DMA((CHUNKS,)),
             pltpu.SemaphoreType.DMA((2,)),
-            *copies,
-            *letters,
+            pltpu.SemaphoreType.DMA((25,)),
+            *[pltpu.SemaphoreType.DMA] * 6,
         ],
         compiler_params=pltpu.CompilerParams(collective_id=0, has_side_effects=True, vmem_limit_bytes=60 * 2**20),
         name="nearest_earlier",

time: 69.4 us -> 68.5 us (0.987)
  Pallas kernels: 68 us -> 67.1 us
    pallas_call x1, Pallas kernels: 68 us -> 67.1 us  [shards(): pl.pallas_call(kernel, out_shape=jax.ShapeDtypeStruct((2, HALF), jnp.floa...]
where the time goes in v5:
time: 68.5 us; the launch traced here: 68.4 us
  Pallas kernels  67.1 us (98%)
  local copies, waits for them, and re-layouts  1.24 us (2%)
    pallas_call x1, Pallas kernels, shards(): pl.pallas_call(kernel, out_shape=jax.ShapeDtypeStruct((2, HALF), jnp.floa...  67.1 us

profile of v5, /device:TPU:1, one launch (start us, length us, event | category | flops | bytes accessed | tf_op | source)
XLA Modules:
  0.0 68.4 jit_solution(6040783695160424465)
XLA Ops:
  0.0 67.1 %nearest_earlier.1 = f32[2,128]{1,0:T(2,128)} custom-call(bf16[256,4096]{1,0:T(8,128)(2,1)} %rows_hbm.1, s32[2,128]{1,0:T(2,128)} %bitcast.3, s32[4]{0:T(128)} %count_hbm.1), custom_call_target="tpu_custom_call" | custom-call | tf_op jit(solution)/shard_map/nearest_earlier/pallas_call | solution.py:345
  67.1 1.2 %copy.5 = f32[256]{0:T(256)} copy(f32[256]{0:T(256)} %bitcast.2) | data formatting | bytes 2048

commit v6 on v5

--- a/solution.py
+++ b/solution.py
@@ -13,10 +13,10 @@
 CHUNKS = ROWS // CHUNK
 ORDER = (2, 3, 0, 1)
 EMPTY = 1 << 20
-OTHER, NEAR, OTHER_LAST, FAR, RELAY = 4, 7, 8, 9, 10
+OTHER, NEAR, FAR, OTHER_LAST, RELAY = 4, 7, 8, 9, 10
 SLOTS = 11
 OTHERS = (OTHER, OTHER + 1, OTHER + 2, OTHER_LAST)
-TURNED = 4 * ROWS
+TURNED = 5 * ROWS
 
 
 def kernel(
@@ -55,8 +55,8 @@
     for copy in words:
         copy.start()
 
-    greeted = [device(i, 0) for i in (1, 2, 3)] + [device(0, i) for i in (1, 2, 3)]
-    greeted += [partner, across, ahead, behind] + [device(i, 0, True) for i in (1, 2, 3)] + [device(0, i, True) for i in (1, 2, 3)]
+    greeted = [device(1, 0), device(-1, 0), device(0, -1), partner, across, behind, device(2, 0), device(0, -2)]
+    greeted += [device(0, i, True) for i in (1, 2, 3)]
     barrier = pltpu.get_barrier_semaphore()
     for there in greeted:
         pl.semaphore_signal(barrier, inc=1, device_id=there, device_id_type=MESH)
@@ -260,10 +260,11 @@
     @pl.when(far_here)
     def _():
         await_chunk(FAR, 0, CHUNKS)
+        turn(FAR, turned, 4 * ROWS)
 
         @pl.loop(0, 2)
         def _(a):
-            meet(a, FAR)
+            meet_turned(a, 0, ROWS, turned, 4 * ROWS, ROWS, 2 * FAR)
 
     await_main(7)
     meet_turned(2, 0, HALF, turned_own, 0, HALF, 0)
@@ -276,9 +277,10 @@
 
     @pl.when(far_here)
     def _():
-        meet(2, FAR)
-
-    meet_turned(3, 0, HALF, turned, 0, TURNED, 2 * OTHER)
+        meet_turned(2, 0, ROWS, turned, 4 * ROWS, ROWS, 2 * FAR)
+        meet_turned(3, 0, HALF, turned, 4 * ROWS, ROWS, 2 * FAR)
+
+    meet_turned(3, 0, HALF, turned, 0, 4 * ROWS, 2 * OTHER)
     for slot in (0, 1, 2):
         fold(slot)
 
@@ -299,14 +301,16 @@
     post(1, 2)
     await_main(8)
     await_up(ORDER[1])
-    meet_turned(3, HALF, HALF, turned, 0, TURNED, 2 * OTHER)
-    post(OTHER, OTHER + 1, OTHER + 2, NEAR)
 
     @pl.when(far_here)
     def _():
-        meet(3, FAR)
-
-    post(FAR)
+        meet_turned(3, HALF, HALF, turned, 0, TURNED, 2 * OTHER)
+
+    @pl.when(jnp.logical_not(far_here))
+    def _():
+        meet_turned(3, HALF, HALF, turned, 0, 4 * ROWS, 2 * OTHER)
+
+    post(OTHER, OTHER + 1, OTHER + 2, NEAR, FAR)
     await_chunk(OTHER_LAST, 0, CHUNKS // 2)
     meet(3, OTHER_LAST, other_rows=HALF)
     fold(3, (0,))

time: 68.5 us -> 67.9 us (level)
  no operation moved by 1% of the time
where the time goes in v6:
time: 67.9 us; the launch traced here: 67.8 us
  Pallas kernels  66.6 us (98%)
  local copies, waits for them, and re-layouts  1.24 us (2%)
    pallas_call x1, Pallas kernels, shards(): pl.pallas_call(kernel, out_shape=jax.ShapeDtypeStruct((2, HALF), jnp.floa...  66.6 us

profile of v6, /device:TPU:1, one launch (start us, length us, event | category | flops | bytes accessed | tf_op | source)
XLA Modules:
  0.0 67.8 jit_solution(1419234260253339119)
XLA Ops:
  0.0 66.6 %nearest_earlier.1 = f32[2,128]{1,0:T(2,128)} custom-call(bf16[256,4096]{1,0:T(8,128)(2,1)} %rows_hbm.1, s32[2,128]{1,0:T(2,128)} %bitcast.3, s32[4]{0:T(128)} %count_hbm.1), custom_call_target="tpu_custom_call" | custom-call | tf_op jit(solution)/shard_map/nearest_earlier/pallas_call | solution.py:349
  66.6 1.2 %copy.5 = f32[256]{0:T(256)} copy(f32[256]{0:T(256)} %bitcast.2) | data formatting | bytes 2048

commit v7 on v6

--- a/solution.py
+++ b/solution.py
@@ -130,15 +130,14 @@
     rank = jnp.where(live, order[...], EMPTY)
     rank_lane[pair(0)] = jnp.broadcast_to(rank[:, None, :], (2, 8, HALF))
     pl.semaphore_wait(barrier, len(greeted))
+    for slot, there in rank_to:
+        rank_copy(slot, there).start()
     for k, c in enumerate(ORDER):
         if k:
             normalise(c)
         send(0, 1, c, down)
         send(0, NEAR, c, side_up)
         send(0, OTHER, c, partner)
-        if k == 0:
-            for slot, there in rank_to:
-                rank_copy(slot, there).start()
 
     best_row[...] = jnp.full_like(best_row, -1.0)
     best_lane[...] = jnp.full_like(best_lane, -1.0)

time: 67.9 us -> 68 us (level)
  no operation moved by 1% of the time
where the time goes in v7:
time: 68 us; the launch traced here: 67.8 us
  Pallas kernels  66.6 us (98%)
  local copies, waits for them, and re-layouts  1.24 us (2%)
    pallas_call x1, Pallas kernels, shards(): pl.pallas_call(kernel, out_shape=jax.ShapeDtypeStruct((2, HALF), jnp.floa...  66.6 us

profile of v7, /device:TPU:1, one launch (start us, length us, event | category | flops | bytes accessed | tf_op | source)
XLA Modules:
  0.0 67.8 jit_solution(3345463409202021370)
XLA Ops:
  0.0 66.6 %nearest_earlier.1 = f32[2,128]{1,0:T(2,128)} custom-call(bf16[256,4096]{1,0:T(8,128)(2,1)} %rows_hbm.1, s32[2,128]{1,0:T(2,128)} %bitcast.3, s32[4]{0:T(128)} %count_hbm.1), custom_call_target="tpu_custom_call" | custom-call | tf_op jit(solution)/shard_map/nearest_earlier/pallas_call | solution.py:348
  66.6 1.2 %copy.5 = f32[256]{0:T(256)} copy(f32[256]{0:T(256)} %bitcast.2) | data formatting | bytes 2048
